TPU v7x, 1024 devices: a whole 8x8x8 slice. The times are simulated.
1024 devices in a mesh: section: 8 (over y_lo, core), expert: 64 (over z, x), dp: 2 (over y_hi).
Axes of the slice: x: 8, y: 8 (y_hi: 2, y_lo: 4; y = y_hi * 4 + y_lo), z: 8, core: 2. Of those that a mesh axis runs over, the one named last changes fastest.
Arguments:
- carry: bfloat16 [16, 2, 4096, 1440], P('section', 'dp', 'expert'), may hold values from -6 to 6
- hidden_fwd: bfloat16 [8, 2, 64, 320, 1440], P('section', 'dp', 'expert'), may hold values from -6 to 6
- expert_weight: bfloat16 [8, 64, 1440, 1440], P('section', 'expert'), may hold values from -0.15625 to 0.15625
- expert_bias: bfloat16 [8, 64, 1440], P('section', 'expert'), may hold values from -3 to 3
- ids_fwd: int32 [8, 2, 4096, 4], P('section', 'dp', 'expert'), may hold values from 0 to 63, all different within a row; in each aligned block of 64 rows (0 to 63, 64 to 127, ..., all dimensions but the last counted through in order) at most 5 rows name the same one
- gates_fwd: float32 [8, 2, 4096, 4], P('section', 'dp', 'expert'), may hold values from 0.05 to 1
- ids_bwd: int32 [8, 2, 4096, 4], P('section', 'dp', 'expert'), may hold values from 0 to 63, all different within a row; in each aligned block of 64 rows (0 to 63, 64 to 127, ..., all dimensions but the last counted through in order) at most 5 rows name the same one
- gates_bwd: float32 [8, 2, 4096, 4], P('section', 'dp', 'expert'), may hold values from 0.05 to 1
Outputs:
- section_out: bfloat16 [8, 2, 4096, 1440], P('section', 'dp', 'expert')
- bias_grad: float32 [8, 64, 1440], P('section', 'expert', 'dp')
Inputs may be any that keep to these rules, and one draw needn't show every extreme that they name: `ids_fwd`: each row names 4 different experts. Among the 64 rows of one device no expert is named more than 5 times, and in every draw some device names some expert exactly 5 times. `ids_bwd`: as for ids_fwd.
All inputs are finite; a program needn't handle non-finite values.
Results may differ from a plain program's by a relative error of at most 0.0085.
Values may be sent and summed in bfloat16 or wider, within the bound.
A program may use at most 32 MiB of HBM per device.

v0:
```python
import jax
import jax.numpy as jnp
from jax import lax
from jax.sharding import PartitionSpec as P


def padded(shard, sides, width):
    for axis, dim in sides:
        devices, length = (lax.axis_size(axis), shard.shape[dim])
        up = [(i, (i + 1) % devices) for i in range(devices)]
        down = [(j, i) for i, j in up]
        last = lax.slice_in_dim(shard, length - width, length, axis=dim)
        initial = lax.slice_in_dim(shard, 0, width, axis=dim)
        before = lax.ppermute(last, axis, up)
        after = lax.ppermute(initial, axis, down)
        shard = jnp.concatenate([before, shard, after], axis=dim)
    return shard


def positions(ids, experts, capacity):
    flat_ids = ids.reshape(-1)
    onehot = (flat_ids[:, None] == jnp.arange(experts, dtype=jnp.int32)).astype(jnp.int32)
    before = jnp.cumsum(onehot, axis=0, dtype=jnp.int32) - onehot
    slot_rank = jnp.sum(before * onehot, axis=1, dtype=jnp.int32)
    return flat_ids * capacity + slot_rank


def on_device(
    carry, hidden_fwd, expert_weight, expert_bias, ids_fwd, gates_fwd, ids_bwd, gates_bwd
):
    extended = padded(carry, (("section", 0),), 1)
    incoming = extended[0, 0]
    upstream = extended[3, 0]
    tok_rows, width = incoming.shape
    experts = lax.axis_size("expert")
    capacity = hidden_fwd.shape[3] // experts
    choose = ids_bwd.shape[3]
    scaled = (gates_bwd[0, 0][:, :, None] * upstream[:, None, :].astype(jnp.float32)).astype(
        jnp.bfloat16
    )
    scaled = scaled.reshape(tok_rows * choose, width)
    place_bwd = positions(ids_bwd[0, 0], experts, capacity)
    buffer = jnp.zeros((experts * capacity, width), jnp.bfloat16).at[place_bwd].set(scaled)
    arrived = lax.all_to_all(buffer, "expert", split_axis=0, concat_axis=0, tiled=True)
    local_total = jnp.sum(arrived, axis=0, dtype=jnp.float32)
    bias_share = lax.psum_scatter(local_total, "dp", scatter_dimension=0, tiled=True)
    produced = jnp.dot(hidden_fwd[0, 0, 0], expert_weight[0, 0], preferred_element_type=jnp.float32)
    produced = (produced + expert_bias[0, 0].astype(jnp.float32)[None, :]).astype(jnp.bfloat16)
    returned = lax.all_to_all(produced, "expert", split_axis=0, concat_axis=0, tiled=True)
    place_fwd = positions(ids_fwd[0, 0], experts, capacity)
    picked = returned[place_fwd].reshape(tok_rows, choose, width)
    mixture = incoming.astype(jnp.float32) + jnp.einsum(
        "tk,tkd->td", gates_fwd[0, 0], picked.astype(jnp.float32)
    )
    return (mixture.astype(jnp.bfloat16)[None, None], bias_share[None, None])


def solution(mesh):
    placed = (
        P("section", "dp", "expert", None),
        P("section", "dp", "expert", None, None),
        P("section", "expert", None, None),
        P("section", "expert", None),
        P("section", "dp", "expert", None),
        P("section", "dp", "expert", None),
        P("section", "dp", "expert", None),
        P("section", "dp", "expert", None),
    )
    return jax.shard_map(
        on_device,
        mesh=mesh,
        in_specs=placed,
        out_specs=(P("section", "dp", "expert", None), P("section", "expert", "dp")),
        check_vma=False,
    )
```

profile of v0, /device:TPU:112, one launch (start us, length us, event | category | flops | bytes accessed | tf_op | source)
XLA Modules:
  0.0 129.8 jit_solution(17137654121767876439)
XLA Ops:
  0.6 0.8 convert_reduce_fusion.1
  1.9 3.9 %fusion.5 = bf16[320,1440]{1,0:T(8,128)(2,1)S(1)} fusion(bf16[1,1,1440,1440]{3,2,1,0:T(8,128)(2,1)} %param.10, bf16[1,1,1,320,1440]{4,3,2,1,0:T(8,128)(2,1)S(1)} %copy-done, f32[1440]{0:T(1024)S(1)} %convert_reduce_fusion.1), kind=kOutput, calls=%fused_computation.6 | convolution fusion | flops 1328025600 | bytes 5996160 | tf_op jit(solution)/shard_map/dot_general | solution.py:47
  5.8 1.4 %all_to_all.14 = bf16[64,5,1440]{2,1,0:T(8,128)(2,1)} reshape(bf16[320,1440]{1,0:T(8,128)(2,1)S(1)} %fusion.5) | data formatting | bytes 1843200 | tf_op jit(solution)/shard_map/all_to_all | solution.py:49
  7.2 22.7 %all-to-all-start = ((bf16[64,5,1440]{2,1,0:T(8,128)(2,1)}), bf16[64,5,1440]{2,1,0:T(8,128)(2,1)S(1)}, u32[]{:S(2)}, u32[]{:S(2)}) async-start(bf16[64,5,1440]{2,1,0:T(8,128)(2,1)} %all_to_all.14), calls=%async_computation | async-start | bytes 3145728 | tf_op jit(solution)/shard_map/all_to_all | solution.py:49
  30.0 0.7 fusion.22
  30.7 2.3 %collective-permute-start.1 = (bf16[1,1,64,1440]{3,2,1,0:T(8,128)(2,1)S(1)}, bf16[1,1,64,1440]{3,2,1,0:T(8,128)(2,1)S(1)}, u32[]{:S(2)}, u32[]{:S(2)}) collective-permute-start(bf16[1,1,64,1440]{3,2,1,0:T(8,128)(2,1)S(1)} %get-tuple-element.2), channel_id=1, source_target_pairs={{128,0},{256,128},{384,256},{512,384},{640,512},{768,640},{896,768... | collective-permute-start | bytes 552968 | tf_op jit(solution)/shard_map/ppermute | solution.py:15
  33.5 0.6 reduce-window.16
  34.7 1.4 %collective-permute-done.1 = bf16[1,1,64,1440]{3,2,1,0:T(8,128)(2,1)S(1)} collective-permute-done((bf16[1,1,64,1440]{3,2,1,0:T(8,128)(2,1)S(1)}, bf16[1,1,64,1440]{3,2,1,0:T(8,128)(2,1)S(1)}, u32[]{:S(2)}, u32[]{:S(2)}) %collective-permute-start.1) | collective-permute-done | bytes 184352 | tf_op jit(solution)/shard_map/ppermute | solution.py:15
  36.2 1.4 %mul.58 = f32[64,4,1440]{2,1,0:T(4,128)} broadcast(f32[64,1440]{1,0:T(8,128)S(1)} %bitcast_convert_fusion), dimensions={0,2} | broadcast | bytes 1843200 | tf_op jit(solution)/shard_map/mul | solution.py:38
  37.6 2.8 %mul.59 = f32[256,1440]{1,0:T(8,128)} reshape(f32[64,4,1440]{2,1,0:T(4,128)} %mul.58) | data formatting | bytes 2949120 | tf_op jit(solution)/shard_map/mul | solution.py:38
  40.3 3.0 %scatter_custom_fusion = bf16[320,1440]{1,0:T(8,128)(2,1)S(1)} fusion(s32[256]{0:T(256)S(1)} %bitcast.88, f32[256,1440]{1,0:T(8,128)} %mul.59, f32[256]{0:T(256)S(1)} %mul.56, bf16[]{:T(256)} %constant.15.clone.1), kind=kCustom, calls=%fused_computation.9 | custom fusion | flops 737280 | bytes 2397186 | tf_op jit(solution)/shard_map/scatter | solution.py:43
  43.4 1.4 %all_to_all.17 = bf16[64,5,1440]{2,1,0:T(8,128)(2,1)} reshape(bf16[320,1440]{1,0:T(8,128)(2,1)S(1)} %scatter_custom_fusion) | data formatting | bytes 1843200 | tf_op jit(solution)/shard_map/all_to_all | solution.py:44
  44.8 26.5 %all-to-all-done = bf16[64,5,1440]{2,1,0:T(8,128)(2,1)S(1)} async-done(((bf16[64,5,1440]{2,1,0:T(8,128)(2,1)}), bf16[64,5,1440]{2,1,0:T(8,128)(2,1)S(1)}, u32[]{:S(2)}, u32[]{:S(2)}) %all-to-all-start) | async-done | bytes 921632 | tf_op jit(solution)/shard_map/all_to_all | solution.py:49
  71.2 7.8 %all-to-all-start.1 = ((bf16[64,5,1440]{2,1,0:T(8,128)(2,1)}), bf16[64,5,1440]{2,1,0:T(8,128)(2,1)}, u32[]{:S(2)}, u32[]{:S(2)}) async-start(bf16[64,5,1440]{2,1,0:T(8,128)(2,1)} %all_to_all.17), calls=%async_computation.1 | async-start | bytes 3145728 | tf_op jit(solution)/shard_map/all_to_all | solution.py:44
  79.1 1.9 %collective-permute-start = (bf16[1,1,64,1440]{3,2,1,0:T(8,128)(2,1)}, bf16[1,1,64,1440]{3,2,1,0:T(8,128)(2,1)}, u32[]{:S(2)}, u32[]{:S(2)}) collective-permute-start(bf16[1,1,64,1440]{3,2,1,0:T(8,128)(2,1)} %get-tuple-element.3), channel_id=1, source_target_pairs={{0,128},{128,256},{256,384},{384,512},{512,640},{640,768},{768,896... | collective-permute-start | bytes 552968 | tf_op jit(solution)/shard_map/ppermute | solution.py:14
  81.6 0.6 reduce-window.14
  82.4 0.7 copy.28
  83.1 1.3 dynamic-slice
  85.2 0.7 all_to_all.16
  85.9 1.3 gather_fusion
  88.5 1.6 %fusion.13 = bf16[1,1,64,1440]{3,2,1,0:T(8,128)(2,1)} fusion(f32[64,1,1440]{2,1,0:T(1,128)S(1)} %fusion.23, bf16[1,1,64,1440]{3,2,1,0:T(8,128)(2,1)} %collective-permute-done), kind=kLoop, calls=%fused_computation.14 | loop fusion | flops 276480 | bytes 737280 | tf_op jit(solution)/shard_map/broadcast_in_dim | solution.py:55
  90.1 28.3 %all-to-all-done.1 = bf16[64,5,1440]{2,1,0:T(8,128)(2,1)} async-done(((bf16[64,5,1440]{2,1,0:T(8,128)(2,1)}), bf16[64,5,1440]{2,1,0:T(8,128)(2,1)}, u32[]{:S(2)}, u32[]{:S(2)}) %all-to-all-start.1) | async-done | bytes 921632 | tf_op jit(solution)/shard_map/all_to_all | solution.py:44
  118.4 1.8 %convert_reduce_fusion = f32[1440]{0:T(1024)S(1)} fusion(bf16[64,5,1440]{2,1,0:T(8,128)(2,1)} %all-to-all-done.1), kind=kLoop, calls=%fused_computation.4 | loop fusion | flops 920160 | bytes 927360 | tf_op jit(solution)/shard_map/reduce_sum | solution.py:45
  120.2 8.9 %all-reduce = f32[1440]{0:T(1024)S(1)} all-reduce(f32[1440]{0:T(1024)S(1)} %convert_reduce_fusion), channel_id=2, replica_groups=mesh['section'=8,'expert'=64,'dp'=2] {'dp'}, use_global_device_ids=true, to_apply=%region_8.9.clone | all-reduce | flops 1440 | bytes 11520
  (47 shorter events, 4.3 us)
Async XLA Ops:
  0.6 1.2 copy-start
  7.2 22.8 %copy-start.1 = (bf16[2,1,64,1440]{3,2,1,0:T(8,128)(2,1)S(1)}, bf16[2,1,64,1440]{3,2,1,0:T(8,128)(2,1)}, u32[]{:S(2)}) copy-start(bf16[2,1,64,1440]{3,2,1,0:T(8,128)(2,1)} %param.8) | copy-start | bytes 1105924
  7.2 25.8 %copy-start.3 = (s32[1,1,64,4]{2,3,1,0:T(4,128)S(1)}, s32[1,1,64,4]{2,3,1,0:T(4,128)}, u32[]{:S(2)}) copy-start(s32[1,1,64,4]{2,3,1,0:T(4,128)} %param.14) | copy-start | bytes 3076
  7.2 27.2 %copy-start.5 = (f32[1,1,64,4]{2,3,1,0:T(4,128)S(1)}, f32[1,1,64,4]{2,3,1,0:T(4,128)}, u32[]{:S(2)}) copy-start(f32[1,1,64,4]{2,3,1,0:T(4,128)} %param.15) | copy-start | bytes 3076
  7.2 64.0 %all-to-all-start = ((bf16[64,5,1440]{2,1,0:T(8,128)(2,1)}), bf16[64,5,1440]{2,1,0:T(8,128)(2,1)S(1)}, u32[]{:S(2)}, u32[]{:S(2)}) async-start(bf16[64,5,1440]{2,1,0:T(8,128)(2,1)} %all_to_all.14), calls=%async_computation | async-start | bytes 3145728 | tf_op jit(solution)/shard_map/all_to_all | solution.py:49
  30.7 5.5 %collective-permute-start.1 = (bf16[1,1,64,1440]{3,2,1,0:T(8,128)(2,1)S(1)}, bf16[1,1,64,1440]{3,2,1,0:T(8,128)(2,1)S(1)}, u32[]{:S(2)}, u32[]{:S(2)}) collective-permute-start(bf16[1,1,64,1440]{3,2,1,0:T(8,128)(2,1)S(1)} %get-tuple-element.2), channel_id=1, source_target_pairs={{128,0},{256,128},{384,256},{512,384},{640,512},{768,640},{896,768... | collective-permute-start | bytes 552968 | tf_op jit(solution)/shard_map/ppermute | solution.py:15
  44.8 36.2 %copy-start.4 = (s32[1,1,64,4]{2,3,1,0:T(4,128)S(1)}, s32[1,1,64,4]{2,3,1,0:T(4,128)}, u32[]{:S(2)}) copy-start(s32[1,1,64,4]{2,3,1,0:T(4,128)} %param.12) | copy-start | bytes 3076
  44.8 37.6 %copy-start.6 = (f32[1,1,64,4]{2,3,1,0:T(4,128)S(1)}, f32[1,1,64,4]{2,3,1,0:T(4,128)}, u32[]{:S(2)}) copy-start(f32[1,1,64,4]{2,3,1,0:T(4,128)} %param.13) | copy-start | bytes 3076
  71.2 47.2 %all-to-all-start.1 = ((bf16[64,5,1440]{2,1,0:T(8,128)(2,1)}), bf16[64,5,1440]{2,1,0:T(8,128)(2,1)}, u32[]{:S(2)}, u32[]{:S(2)}) async-start(bf16[64,5,1440]{2,1,0:T(8,128)(2,1)} %all_to_all.17), calls=%async_computation.1 | async-start | bytes 3145728 | tf_op jit(solution)/shard_map/all_to_all | solution.py:44
  79.1 9.4 %collective-permute-start = (bf16[1,1,64,1440]{3,2,1,0:T(8,128)(2,1)}, bf16[1,1,64,1440]{3,2,1,0:T(8,128)(2,1)}, u32[]{:S(2)}, u32[]{:S(2)}) collective-permute-start(bf16[1,1,64,1440]{3,2,1,0:T(8,128)(2,1)} %get-tuple-element.3), channel_id=1, source_target_pairs={{0,128},{128,256},{256,384},{384,512},{512,640},{640,768},{768,896... | collective-permute-start | bytes 552968 | tf_op jit(solution)/shard_map/ppermute | solution.py:14
  87.2 0.8 copy-start.2
where the time goes:
time: 130 us
  waiting for transfers between devices  56.2 us (43%)
  starting transfers between devices  34.8 us (27%)
  local copies, waits for them, and re-layouts  15.1 us (12%)
  blocking collectives  8.92 us (7%)
  other arithmetic  8.77 us (7%)
  matrix products  4.49 us (3%)
  between operations  1.5 us (1%)
    all_to_all x1, waiting for transfers between devices, on_device(): lax.all_to_all(buffer, 'expert', split_axis=0, concat_axis=0, tiled=True)  28.3 us
    all_to_all x1, waiting for transfers between devices, on_device(): lax.all_to_all(produced, 'expert', split_axis=0, concat_axis=0, tiled=True)  26.5 us
    all_to_all x1, starting transfers between devices, on_device(): lax.all_to_all(produced, 'expert', split_axis=0, concat_axis=0, tiled=True)  22.7 us
    unnamed x1, blocking collectives  8.92 us
    all_to_all x1, starting transfers between devices, on_device(): lax.all_to_all(buffer, 'expert', split_axis=0, concat_axis=0, tiled=True)  7.83 us
    mul x3, local copies, waits for them, and re-layouts, on_device(): gates_bwd[0, 0][:, :, None] * upstream[:, None, :].astype(jnp.float32)  4.3 us
    dot_general x1, matrix products, on_device(): jnp.dot(hidden_fwd[0, 0, 0], expert_weight[0, 0], preferred_element_type=...  3.94 us
    scatter x1, other arithmetic, on_device(): jnp.zeros((experts * capacity, width), jnp.bfloat16).at[place_bwd]  3.01 us
  transfers between devices with their start and end apart: 4, of which 3 were waited for; matrix products, arithmetic and copies ran while one was open for 13% of the time, Pallas kernels for 0%

commit v1 on v0

v1 whole, which is shorter than its diff:
```python
import functools

import jax
import jax.numpy as jnp
from jax import lax
from jax.experimental import pallas as pl
from jax.experimental.pallas import tpu as pltpu
from jax.sharding import PartitionSpec as P

F32 = jnp.float32
BF16 = jnp.bfloat16
SIDE = 8
ROWS = 8
LANES = 128

CHUNKS = ((0, 384, "z"), (768, 384, "x"), (384, 384, "z"), (1152, 288, "x"))


def iota(shape, dim):
    return lax.broadcasted_iota(jnp.int32, shape, dim)


def dot(a, b, dims=((1,), (0,))):
    return lax.dot_general(a, b, (dims, ((), ())), preferred_element_type=F32)


def split(value):
    high = value.astype(BF16)
    return high, (value - high.astype(F32)).astype(BF16)


def table(ids, gates, owner):
    shape = owner.shape
    chosen, weight = jnp.zeros(shape, F32), jnp.zeros(shape, F32)
    for k in range(ids.shape[1]):
        hit = ids[:, k : k + 1] == owner
        chosen = jnp.where(hit, 1.0, chosen)
        weight = jnp.where(hit, gates[:, k : k + 1], weight)
    return chosen, weight


def combine_matrix(chosen, weight, cap, order):
    tokens, experts = chosen.shape
    slots = experts * cap
    earlier = (iota((tokens, tokens), 1) < iota((tokens, tokens), 0)).astype(F32).astype(BF16)
    rank = dot(earlier, chosen.astype(BF16))
    row, column = iota((experts, slots), 0), iota((experts, slots), 1)
    if order == "x":
        row = (row & (SIDE - 1)) * SIDE + (row >> (SIDE.bit_length() - 1))
    inside = column - row * cap
    member = (inside >= 0) & (inside < cap)
    spread = jnp.where(member, 1.0, 0.0).astype(BF16)
    slot = jnp.sum(jnp.where(member, inside, 0).astype(F32), axis=0, keepdims=True)
    hit = (dot(rank.astype(BF16), spread) == slot) & (dot(chosen.astype(BF16), spread) > 0.5)
    high, low = split(weight)
    parts = [jnp.where(hit, dot(part, spread), 0.0) for part in (high, low)]
    return jnp.concatenate(parts, axis=0).astype(BF16)


def kernel(
    cap,
    replicas,
    sections,
    carry,
    hidden,
    weight,
    bias,
    ids_fwd,
    gates_fwd,
    ids_bwd,
    gates_bwd,
    out,
    bias_grad,
    hid_v,
    wgt_v,
    inc_v,
    up_v,
    share,
    share_bf,
    share_in,
    col_out,
    col_in,
    row_out,
    row_in,
    *rest,
):
    n = len(CHUNKS)
    first_out, first_in, second_out, second_in = (rest[i * n : (i + 1) * n] for i in range(4))
    local_sem, send_sem, recv_sem = rest[4 * n :]
    me = lax.axis_index("expert")
    z, x = me // SIDE, me % SIDE
    sec, rep = lax.axis_index("section"), lax.axis_index("dp")
    tokens, width = inc_v.shape
    experts = SIDE * SIDE
    slots = experts * cap
    half = width // replicas
    group = SIDE * cap

    def along(axis, step):
        if axis == "z":
            other = (z + step) % SIDE
            return other, {"expert": other * SIDE + x}
        other = (x + step) % SIDE
        return other, {"expert": z * SIDE + other}

    after, before = (sec + 1) % sections, (sec + sections - 1) % sections

    barrier = pltpu.get_barrier_semaphore()
    partners = [along(axis, d)[1] for axis in "zx" for d in range(1, SIDE)]
    partners += [{"section": after}, {"section": before}, {"dp": 1 - rep}]
    for device in partners:
        pl.semaphore_signal(barrier, inc=1, device_id=device, device_id_type=pl.DeviceIdType.MESH)

    loads = [pltpu.make_async_copy(hidden.at[0, 0, 0], hid_v, local_sem.at[n])]
    for i, (start, size, _) in enumerate(CHUNKS):
        columns = pl.ds(start, size)
        loads.append(
            pltpu.make_async_copy(
                weight.at[0, 0, :, columns], wgt_v.at[:, columns], local_sem.at[i]
            )
        )
    for load in loads:
        load.start()

    def remote(src, dst, sem, device):
        return pltpu.make_async_remote_copy(
            src_ref=src,
            dst_ref=dst,
            send_sem=send_sem.at[sem],
            recv_sem=recv_sem.at[sem],
            device_id=device,
            device_id_type=pl.DeviceIdType.MESH,
        )

    def exchange(axis, src, dst, sem):
        here = z if axis == "z" else x
        copies = []
        for d in range(1, SIDE):
            other, device = along(axis, d)
            copy = remote(src.at[other], dst.at[here], sem + d - 1, device)
            copy.start()
            copies.append(copy)
        dst[here] = src[here]
        return copies

    def arrived(copies):
        for copy in copies:
            copy.wait_recv()

    swap_row, swap_col = iota((slots, slots), 0), iota((slots, slots), 1)
    low_group = sum((swap_row >= group * i).astype(jnp.int32) for i in range(1, SIDE))
    low_rest = swap_row - low_group * group
    inner = sum((low_rest >= cap * i).astype(jnp.int32) for i in range(1, SIDE))
    swap = swap_col == inner * group + low_group * cap + (low_rest - inner * cap)
    swap = jnp.where(swap, 1.0, 0.0).astype(BF16)
    owner = iota((tokens, experts), 1)
    chosen, gate = table(ids_fwd[0, 0], gates_fwd[0, 0], owner)
    combine = {order: combine_matrix(chosen, gate, cap, order) for order in "zx"}
    share[...] = jnp.zeros_like(share)

    def produce(i):
        start, size, axis = CHUNKS[i]
        columns = pl.ds(start, size)
        loads[i + 1].wait()
        block = dot(hid_v[...], wgt_v[:, columns]) + bias[0, :, columns].astype(F32)
        if axis == "x":
            block = dot(swap, block.astype(BF16))
        for other in range(SIDE):
            first_out[i][other] = block[other * group : (other + 1) * group].astype(BF16)

    def gathered(ref):
        return ref[...].reshape(slots, ref.shape[2])

    def turn(i):
        block = dot(swap, gathered(first_in[i]))
        for other in range(SIDE):
            second_out[i][other] = block[other * group : (other + 1) * group].astype(BF16)

    per = SIDE - 1
    first_sem = [i * per for i in range(n)]
    second_sem = [(n + i) * per for i in range(n)]
    col_sem, row_sem = 2 * n * per, (2 * n + 1) * per
    up_sem = (2 * n + 2) * per
    inc_sem, share_sem = up_sem + 1, up_sem + 2
    first, second = [None] * n, [None] * n
    other_axis = {"z": "x", "x": "z"}

    loads[0].wait()
    produce(0)
    pl.semaphore_wait(barrier, len(partners))
    first[0] = exchange(CHUNKS[0][2], first_out[0], first_in[0], first_sem[0])
    up_copy = remote(carry.at[0, 0], up_v, up_sem, {"section": before})
    up_copy.start()
    for i in range(1, n):
        produce(i)
        first[i] = exchange(CHUNKS[i][2], first_out[i], first_in[i], first_sem[i])

    owner = (owner & (SIDE - 1)) * SIDE + (owner >> (SIDE.bit_length() - 1))
    _, gate = table(ids_bwd[0, 0], gates_bwd[0, 0], owner)
    high, low = split(gate)
    up_copy.wait_recv()
    upstream = up_v[...]
    total = dot(high, upstream, ((0,), (0,))) + dot(low, upstream, ((0,), (0,)))
    for h in range(replicas):
        share[h, :, 0:half] = total[:, h * half : (h + 1) * half]
    share_bf[...] = share[1 - rep].astype(BF16)
    share_copy = remote(share_bf, share_in, share_sem, {"dp": 1 - rep})
    share_copy.start()
    inc_copy = remote(carry.at[1, 0], inc_v, inc_sem, {"section": after})
    inc_copy.start()

    def second_phase(i):
        arrived(first[i])
        turn(i)
        axis = other_axis[CHUNKS[i][2]]
        second[i] = exchange(axis, second_out[i], second_in[i], second_sem[i])

    second_phase(0)
    second_phase(1)

    share_copy.wait_recv()
    both = share[rep] + share_in[...].astype(F32)
    part = both.shape[1] // 2
    for other in range(SIDE):
        rows = both[other * SIDE : (other + 1) * SIDE]
        col_out[other] = jnp.concatenate([rows[:, :part], rows[:, part:]], axis=0).astype(BF16)
    col_copies = exchange("x", col_out, col_in, col_sem)

    for i in range(2, n):
        second_phase(i)

    arrived(col_copies)
    both = jnp.sum(col_in[...].astype(F32), axis=0)
    tiles = part // LANES
    for other in range(SIDE):
        for h in range(2):
            for tile in range(tiles):
                row_out[other, h * tiles + tile : h * tiles + tile + 1, :] = both[
                    h * SIDE + other : h * SIDE + other + 1, tile * LANES : (tile + 1) * LANES
                ]
    row_copies = exchange("z", row_out, row_in, row_sem)

    def finish(i):
        start, size, axis = CHUNKS[i]
        arrived(second[i])
        mixed = dot(combine[other_axis[axis]], gathered(second_in[i]))
        mixed = mixed[:tokens] + mixed[tokens:] + inc_v[:, start : start + size].astype(F32)
        out[0, 0, :, start : start + size] = mixed.astype(BF16)

    inc_copy.wait_recv()
    finish(0)
    finish(1)
    arrived(row_copies)
    mine = jnp.sum(row_in[...], axis=0)
    for tile in range(pl.cdiv(half, LANES)):
        size = min(LANES, half - tile * LANES)
        bias_grad[0, :, tile * LANES : tile * LANES + size] = mine[tile : tile + 1, :size]
    for i in range(2, n):
        finish(i)

    copies = [up_copy, inc_copy, share_copy, *col_copies, *row_copies]
    for group_of in first + second:
        copies += group_of
    for copy in copies:
        copy.wait_send()


def solution(mesh):
    sections, replicas = mesh.shape["section"], mesh.shape["dp"]

    def step(carry, hidden, weight, bias, ids_fwd, gates_fwd, ids_bwd, gates_bwd):
        tokens, width = carry.shape[2:]
        slots, depth = hidden.shape[3:]
        experts = mesh.shape["expert"]
        cap = slots // experts
        half = width // replicas
        wide = pl.cdiv(half, 2 * LANES) * 2 * LANES
        blocks = [pltpu.VMEM((SIDE, SIDE * cap, size), BF16) for _, size, _ in CHUNKS]
        messages = (2 * len(CHUNKS) + 2) * (SIDE - 1) + 3
        in_hbm, in_vmem = pl.BlockSpec(memory_space=pl.ANY), pl.BlockSpec(memory_space=pltpu.VMEM)
        return pl.pallas_call(
            functools.partial(kernel, cap, replicas, sections),
            out_shape=(
                jax.ShapeDtypeStruct((1, 1, tokens, width), BF16),
                jax.ShapeDtypeStruct((1, 1, half), F32),
            ),
            in_specs=[in_hbm] * 3 + [in_vmem] * 5,
            out_specs=(in_vmem, in_vmem),
            scratch_shapes=[
                pltpu.VMEM((slots, depth), BF16),
                pltpu.VMEM((depth, width), BF16),
                pltpu.VMEM((tokens, width), BF16),
                pltpu.VMEM((tokens, width), BF16),
                pltpu.VMEM((replicas, experts, wide), F32),
                pltpu.VMEM((experts, wide), BF16),
                pltpu.VMEM((experts, wide), BF16),
                pltpu.VMEM((SIDE, 2 * SIDE, wide // 2), BF16),
                pltpu.VMEM((SIDE, 2 * SIDE, wide // 2), BF16),
                pltpu.VMEM((SIDE, ROWS, LANES), F32),
                pltpu.VMEM((SIDE, ROWS, LANES), F32),
                *(blocks * 4),
                pltpu.SemaphoreType.DMA((len(CHUNKS) + 1,)),
                pltpu.SemaphoreType.DMA((messages,)),
                pltpu.SemaphoreType.DMA((messages,)),
            ],
            compiler_params=pltpu.CompilerParams(
                collective_id=0, has_side_effects=True, vmem_limit_bytes=48 * 2**20
            ),
            cost_estimate=pl.CostEstimate(
                flops=2 * slots * depth * width,
                bytes_accessed=2 * (depth * width + slots * depth + 4 * tokens * width),
                transcendentals=0,
            ),
        )(carry, hidden, weight, bias, ids_fwd, gates_fwd, ids_bwd, gates_bwd)

    placed = (
        P("section", "dp", "expert", None),
        P("section", "dp", "expert", None, None),
        P("section", "expert", None, None),
        P("section", "expert", None),
        P("section", "dp", "expert", None),
        P("section", "dp", "expert", None),
        P("section", "dp", "expert", None),
        P("section", "dp", "expert", None),
    )
    return jax.shard_map(
        step,
        mesh=mesh,
        in_specs=placed,
        out_specs=(P("section", "dp", "expert", None), P("section", "expert", "dp")),
        check_vma=False,
    )
```

time: 130 us -> 61.8 us (0.48)
  the two profiles are of different devices: /device:TPU:112 before, /device:TPU:16 now
where the time goes in v1:
time: 61.8 us; the launch traced here: 61.4 us
  Pallas kernels  51.2 us (83%)
  local copies, waits for them, and re-layouts  9.48 us (15%)
  between operations  0.64 us (1%)
    pallas_call x1, Pallas kernels, step(): pl.pallas_call(functools.partial(kernel, cap, replicas, sections), out_sh...  51.2 us
    unnamed x14, local copies, waits for them, and re-layouts  9.48 us

profile of v1, /device:TPU:16, one launch (start us, length us, event | category | flops | bytes accessed | tf_op | source)
XLA Modules:
  0.0 61.4 jit_solution(18050819033689396103)
XLA Ops:
  0.6 0.8 %copy.10.ids_fwd = s32[1,1,64,4]{3,2,1,0:T(8,128)S(1)} copy(s32[1,1,64,4]{2,3,1,0:T(4,128)} %param.12) | data formatting | bytes 2048 | tf_op args[4]
  1.4 0.8 %copy.11.gates_fwd = f32[1,1,64,4]{3,2,1,0:T(8,128)S(1)} copy(f32[1,1,64,4]{2,3,1,0:T(4,128)} %param.13) | data formatting | bytes 2048 | tf_op args[5]
  2.2 0.8 %copy.12.ids_bwd = s32[1,1,64,4]{3,2,1,0:T(8,128)S(1)} copy(s32[1,1,64,4]{2,3,1,0:T(4,128)} %param.14) | data formatting | bytes 2048 | tf_op args[6]
  2.9 0.8 %copy.13.gates_bwd = f32[1,1,64,4]{3,2,1,0:T(8,128)S(1)} copy(f32[1,1,64,4]{2,3,1,0:T(4,128)} %param.15) | data formatting | bytes 2048 | tf_op args[7]
  3.7 0.0 copy-start
  3.7 2.3 %copy-done = bf16[1,1,1440,1440]{3,2,1,0:T(8,128)(2,1)S(1)} copy-done((bf16[1,1,1440,1440]{3,2,1,0:T(8,128)(2,1)S(1)}, bf16[1,1,1440,1440]{3,2,1,0:T(8,128)(2,1)}, u32[]{:S(2)}) %copy-start) | copy-done | bytes 4147224
  6.0 0.0 copy-start.1
  6.0 1.2 %copy-done.1 = bf16[1,1,1,320,1440]{4,3,2,1,0:T(8,128)(2,1)S(1)} copy-done((bf16[1,1,1,320,1440]{4,3,2,1,0:T(8,128)(2,1)S(1)}, bf16[1,1,1,320,1440]{4,3,2,1,0:T(8,128)(2,1)}, u32[]{:S(2)}) %copy-start.1) | copy-done | bytes 921624
  7.2 0.0 copy-start.2
  7.2 1.0 %copy-done.2 = bf16[2,1,64,1440]{3,2,1,0:T(8,128)(2,1)S(1)} copy-done((bf16[2,1,64,1440]{3,2,1,0:T(8,128)(2,1)S(1)}, bf16[2,1,64,1440]{3,2,1,0:T(8,128)(2,1)}, u32[]{:S(2)}) %copy-start.2) | copy-done | bytes 368664
  8.2 0.0 copy-start.3
  8.2 0.7 %copy-done.3 = bf16[1,1,1440]{2,1,0:T(2,128)(2,1)S(1)} copy-done((bf16[1,1,1440]{2,1,0:T(2,128)(2,1)S(1)}, bf16[1,1,1440]{2,1,0:T(2,128)(2,1)}, u32[]{:S(2)}) %copy-start.3) | copy-done | bytes 2904
  8.9 51.2 %shard_map.95 = (bf16[1,1,64,1440]{3,2,1,0:T(8,128)(2,1)S(1)}, f32[1,1,720]{2,1,0:T(1,128)S(1)}) custom-call(bf16[2,1,64,1440]{3,2,1,0:T(8,128)(2,1)S(1)} %copy-done.2, bf16[1,1,1,320,1440]{4,3,2,1,0:T(8,128)(2,1)S(1)} %copy-done.1, bf16[1,1,1440,1440]{3,2,1,0:T(8,128)(2,1)S(1)} %copy-done, bf16[1,1,1440]{2,1,0:T(2,128)(2,1)S(1)} %copy-done.3, ...), custom_call_target="tpu_custom_call" | custom-call | flops 1327104000 | bytes 5806080 | tf_op jit(solution)/shard_map/pallas_call | solution.py:281
  60.1 0.7 %copy.16 = bf16[1,1,64,1440]{3,2,1,0:T(8,128)(2,1)} copy(bf16[1,1,64,1440]{3,2,1,0:T(8,128)(2,1)S(1)} %get-tuple-element.4) | data formatting | bytes 368640
  60.8 0.6 copy.17
Async XLA Ops:
  3.7 2.3 %copy-start = (bf16[1,1,1440,1440]{3,2,1,0:T(8,128)(2,1)S(1)}, bf16[1,1,1440,1440]{3,2,1,0:T(8,128)(2,1)}, u32[]{:S(2)}) copy-start(bf16[1,1,1440,1440]{3,2,1,0:T(8,128)(2,1)} %weight.1) | copy-start | bytes 12441604
  6.0 1.2 %copy-start.1 = (bf16[1,1,1,320,1440]{4,3,2,1,0:T(8,128)(2,1)S(1)}, bf16[1,1,1,320,1440]{4,3,2,1,0:T(8,128)(2,1)}, u32[]{:S(2)}) copy-start(bf16[1,1,1,320,1440]{4,3,2,1,0:T(8,128)(2,1)} %hidden.1) | copy-start | bytes 2764804
  7.2 1.0 %copy-start.2 = (bf16[2,1,64,1440]{3,2,1,0:T(8,128)(2,1)S(1)}, bf16[2,1,64,1440]{3,2,1,0:T(8,128)(2,1)}, u32[]{:S(2)}) copy-start(bf16[2,1,64,1440]{3,2,1,0:T(8,128)(2,1)} %carry.1) | copy-start | bytes 1105924
  8.2 0.7 %copy-start.3 = (bf16[1,1,1440]{2,1,0:T(2,128)(2,1)S(1)}, bf16[1,1,1440]{2,1,0:T(2,128)(2,1)}, u32[]{:S(2)}) copy-start(bf16[1,1,1440]{2,1,0:T(2,128)(2,1)} %bias.1) | copy-start | bytes 8644

commit v2 on v1

v2 whole, which is shorter than its diff:
```python
import functools

import jax
import jax.numpy as jnp
from jax import lax
from jax.experimental import pallas as pl
from jax.experimental.pallas import tpu as pltpu
from jax.sharding import PartitionSpec as P

F32 = jnp.float32
BF16 = jnp.bfloat16
SIDE = 8
ROWS = 8
LANES = 128

CHUNKS = (
    (0, 256, "z"),
    (768, 256, "x"),
    (256, 256, "z"),
    (1024, 256, "x"),
    (512, 256, "z"),
    (1280, 160, "x"),
)


def iota(shape, dim):
    return lax.broadcasted_iota(jnp.int32, shape, dim)


def dot(a, b, dims=((1,), (0,))):
    return lax.dot_general(a, b, (dims, ((), ())), preferred_element_type=F32)


def swapped(expert):
    return (expert & (SIDE - 1)) * SIDE + (expert >> (SIDE.bit_length() - 1))


def split(value):
    high = value.astype(BF16)
    return high, (value - high.astype(F32)).astype(BF16)


def table(ids, gates, owner):
    shape = owner.shape
    chosen, weight = jnp.zeros(shape, F32), jnp.zeros(shape, F32)
    for k in range(ids.shape[0]):
        hit = ids[k : k + 1] == owner
        chosen = jnp.where(hit, 1.0, chosen)
        weight = jnp.where(hit, gates[k : k + 1], weight)
    return chosen, weight


def combine_matrix(chosen, weight, cap, order):
    experts, tokens = chosen.shape
    slots = experts * cap
    earlier = (iota((tokens, tokens), 0) < iota((tokens, tokens), 1)).astype(F32).astype(BF16)
    rank = dot(chosen.astype(BF16), earlier)
    row, column = iota((experts, slots), 0), iota((experts, slots), 1)
    if order == "x":
        row = swapped(row)
    inside = column - row * cap
    member = (inside >= 0) & (inside < cap)
    spread = jnp.where(member, 1.0, 0.0).astype(BF16)
    slot = jnp.sum(jnp.where(member, inside, 0).astype(F32), axis=0, keepdims=True)

    def widen(part):
        return dot(part.astype(BF16), spread, ((0,), (0,)))

    hit = (widen(rank) == slot) & (widen(chosen) > 0.5)
    parts = [jnp.where(hit, widen(part), 0.0) for part in split(weight)]
    return jnp.concatenate(parts, axis=0).astype(BF16)


def kernel(
    cap,
    replicas,
    sections,
    carry,
    hidden,
    weight,
    bias,
    ids_fwd,
    gates_fwd,
    ids_bwd,
    gates_bwd,
    out_to,
    bias_to,
    out,
    bias_grad,
    hid_v,
    wgt_v,
    bias_v,
    ids_v,
    gates_v,
    inc_v,
    grad_v,
    grad_out,
    grad_in,
    peer_ids,
    peer_gates,
    col_out,
    col_in,
    row_out,
    row_in,
    *rest,
):
    n = len(CHUNKS)
    first_out, first_in, second_out, second_in = (rest[i * n : (i + 1) * n] for i in range(4))
    local_sem, store_sem, send_sem, recv_sem = rest[4 * n :]
    me = lax.axis_index("expert")
    z, x = me // SIDE, me % SIDE
    sec, rep = lax.axis_index("section"), lax.axis_index("dp")
    tokens, width = inc_v.shape
    experts = SIDE * SIDE
    slots = experts * cap
    half = width // replicas
    group = SIDE * cap

    def along(axis, step):
        if axis == "z":
            other = (z + step) % SIDE
            return other, {"expert": other * SIDE + x}
        other = (x + step) % SIDE
        return other, {"expert": z * SIDE + other}

    after, before = (sec + 1) % sections, (sec + sections - 1) % sections

    barrier = pltpu.get_barrier_semaphore()
    partners = [along(axis, d)[1] for axis in "zx" for d in range(1, SIDE)]
    other_rep = {"dp": 1 - rep}
    partners += [{"section": s} | d for s in (after, before) for d in ({}, other_rep)]
    partners += [other_rep]
    for device in partners:
        pl.semaphore_signal(barrier, inc=1, device_id=device, device_id_type=pl.DeviceIdType.MESH)

    loads = [pltpu.make_async_copy(hidden.at[0, 0, 0], hid_v, local_sem.at[n])]
    small = [
        pltpu.make_async_copy(src.at[at], dst, local_sem.at[n + 1 + i])
        for i, (src, at, dst) in enumerate(
            (
                (bias, 0, bias_v),
                (carry, (0, 0), grad_v),
                (ids_fwd, (0, 0), ids_v.at[0]),
                (ids_bwd, (0, 0), ids_v.at[1]),
                (gates_fwd, (0, 0), gates_v.at[0]),
                (gates_bwd, (0, 0), gates_v.at[1]),
            )
        )
    ]
    for i, (start, size, _) in enumerate(CHUNKS):
        columns = pl.ds(start, size)
        loads.append(
            pltpu.make_async_copy(
                weight.at[0, 0, :, columns], wgt_v.at[:, columns], local_sem.at[i]
            )
        )
    for load in small[:2] + loads[:2] + small[2:] + loads[2:]:
        load.start()

    def remote(src, dst, sem, device):
        return pltpu.make_async_remote_copy(
            src_ref=src,
            dst_ref=dst,
            send_sem=send_sem.at[sem],
            recv_sem=recv_sem.at[sem],
            device_id=device,
            device_id_type=pl.DeviceIdType.MESH,
        )

    def exchange(axis, src, dst, sem):
        here = z if axis == "z" else x
        copies = []
        for d in farthest_first:
            other, device = along(axis, d)
            copy = remote(src.at[other], dst.at[here], sem + d - 1, device)
            copy.start()
            copies.append(copy)
        dst[here] = src[here]
        return copies

    farthest_first = sorted(range(1, SIDE), key=lambda d: -min(d, SIDE - d))

    @jax.named_scope("arrive")
    def arrived(copies):
        for copy in copies:
            copy.wait_recv()

    swap_row, swap_col = iota((slots, slots), 0), iota((slots, slots), 1)
    low_group = sum((swap_row >= group * i).astype(jnp.int32) for i in range(1, SIDE))
    low_rest = swap_row - low_group * group
    inner = sum((low_rest >= cap * i).astype(jnp.int32) for i in range(1, SIDE))
    swap = swap_col == inner * group + low_group * cap + (low_rest - inner * cap)
    swap = jnp.where(swap, 1.0, 0.0).astype(BF16)

    @jax.named_scope("produce")
    def produce(i):
        start, size, axis = CHUNKS[i]
        columns = pl.ds(start, size)
        loads[i + 1].wait()
        block = dot(hid_v[...], wgt_v[:, columns]) + bias_v[:, columns].astype(F32)
        if axis == "x":
            block = dot(swap, block.astype(BF16))
        for other in range(SIDE):
            first_out[i][other] = block[other * group : (other + 1) * group].astype(BF16)

    def gathered(ref):
        return ref[...].reshape(slots, ref.shape[2])

    @jax.named_scope("turn")
    def turn(i):
        block = dot(swap, gathered(first_in[i]))
        for other in range(SIDE):
            second_out[i][other] = block[other * group : (other + 1) * group].astype(BF16)

    per = SIDE - 1
    first_sem = [i * per for i in range(n)]
    second_sem = [(n + i) * per for i in range(n)]
    col_sem, row_sem = 2 * n * per, (2 * n + 1) * per
    up_sem = (2 * n + 2) * per
    inc_sem = up_sem + 4
    first, second = [None] * n, [None] * n
    other_axis = {"z": "x", "x": "z"}

    small[1].wait()
    for h in range(replicas):
        part = grad_v[:, h * half : (h + 1) * half]
        blank = jnp.zeros((tokens, grad_out.shape[2] - half), BF16)
        grad_out[h] = jnp.concatenate([part, blank], axis=1)
    loads[0].wait()
    small[0].wait()
    produce(0)
    with jax.named_scope("greet"):
        pl.semaphore_wait(barrier, len(partners))
    grad_copies = [
        remote(grad_out.at[1 - rep], grad_in.at[1], up_sem + 1, {"section": before} | other_rep),
        remote(grad_out.at[rep], grad_in.at[0], up_sem, {"section": before}),
        remote(ids_bwd.at[0, 0], peer_ids, up_sem + 2, other_rep),
        remote(gates_bwd.at[0, 0], peer_gates, up_sem + 3, other_rep),
    ]
    for copy in grad_copies:
        copy.start()
    first[0] = exchange(CHUNKS[0][2], first_out[0], first_in[0], first_sem[0])
    for i in range(1, n):
        produce(i)
        first[i] = exchange(CHUNKS[i][2], first_out[i], first_in[i], first_sem[i])

    for load in small[2:]:
        load.wait()
    owner = iota((experts, tokens), 0)
    with jax.named_scope("upstream"):
        arrived(grad_copies)
    inc_copy = remote(carry.at[1, 0], inc_v, inc_sem, {"section": after})
    inc_copy.start()
    total = jnp.zeros((experts, grad_in.shape[2]), F32)
    for i, (ids, gates) in enumerate(((ids_v[1], gates_v[1]), (peer_ids[...], peer_gates[...]))):
        _, gate = table(ids, gates, swapped(owner))
        for part in split(gate):
            total = total + dot(part, grad_in[i])
    part = total.shape[1] // 2
    for other in range(SIDE):
        rows = total[other * SIDE : (other + 1) * SIDE]
        col_out[other] = jnp.concatenate([rows[:, :part], rows[:, part:]], axis=0).astype(BF16)
    col_copies = exchange("x", col_out, col_in, col_sem)

    chosen, gate = table(ids_v[0], gates_v[0], owner)
    combine = {order: combine_matrix(chosen, gate, cap, order) for order in "zx"}

    def second_phase(i):
        arrived(first[i])
        turn(i)
        axis = other_axis[CHUNKS[i][2]]
        second[i] = exchange(axis, second_out[i], second_in[i], second_sem[i])

    for i in range(n):
        second_phase(i)

    arrived(col_copies)
    both = jnp.sum(col_in[...].astype(F32), axis=0)
    tiles = part // LANES
    for other in range(SIDE):
        for h in range(2):
            for tile in range(tiles):
                row_out[other, h * tiles + tile : h * tiles + tile + 1, :] = both[
                    h * SIDE + other : h * SIDE + other + 1, tile * LANES : (tile + 1) * LANES
                ]
    row_copies = exchange("z", row_out, row_in, row_sem)

    @jax.named_scope("finish")
    def finish(i):
        start, size, axis = CHUNKS[i]
        arrived(second[i])
        mixed = dot(combine[other_axis[axis]], gathered(second_in[i]))
        mixed = mixed[:tokens] + mixed[tokens:] + inc_v[:, start : start + size].astype(F32)
        out[:, start : start + size] = mixed.astype(BF16)
        store = pltpu.make_async_copy(
            out.at[:, pl.ds(start, size)], out_to.at[0, 0, :, pl.ds(start, size)], store_sem.at[i]
        )
        store.start()
        return store

    inc_copy.wait_recv()
    stores = [finish(i) for i in range(n)]
    arrived(row_copies)
    mine = jnp.sum(row_in[...], axis=0)
    for tile in range(pl.cdiv(half, LANES)):
        size = min(LANES, half - tile * LANES)
        bias_grad[:, tile * LANES : tile * LANES + size] = mine[tile : tile + 1, :size]
    stores.append(pltpu.make_async_copy(bias_grad, bias_to.at[0], store_sem.at[n]))
    stores[n].start()
    copies = [inc_copy, *grad_copies, *col_copies, *row_copies]
    for group_of in first + second:
        copies += group_of
    for copy in copies:
        copy.wait_send()
    for store in stores:
        store.wait()


def hand_over(out, bias_grad, out_to, bias_to, out_v, bias_v, sem):
    steps = [
        (pltpu.make_async_copy(a, v, sem.at[2 * i]), pltpu.make_async_copy(v, b, sem.at[2 * i + 1]))
        for i, (a, v, b) in enumerate(((out, out_v, out_to), (bias_grad, bias_v, bias_to)))
    ]
    for load, _ in steps:
        load.start()
    for load, store in steps:
        load.wait()
        store.start()
    for _, store in steps:
        store.wait()


def solution(mesh):
    sections, replicas = mesh.shape["section"], mesh.shape["dp"]

    def step(carry, hidden, weight, bias, ids_fwd, gates_fwd, ids_bwd, gates_bwd):
        tokens, width = carry.shape[2:]
        slots, depth = hidden.shape[3:]
        experts = mesh.shape["expert"]
        cap = slots // experts
        half = width // replicas
        wide = pl.cdiv(half, 2 * LANES) * 2 * LANES
        blocks = [pltpu.VMEM((SIDE, SIDE * cap, size), BF16) for _, size, _ in CHUNKS]
        messages = (2 * len(CHUNKS) + 2) * (SIDE - 1) + 5
        in_hbm = pl.BlockSpec(memory_space=pltpu.HBM)
        shapes = (
            jax.ShapeDtypeStruct((1, 1, tokens, width), BF16),
            jax.ShapeDtypeStruct((1, 1, half), F32),
        )
        results = pl.pallas_call(
            functools.partial(kernel, cap, replicas, sections),
            out_shape=shapes,
            in_specs=[in_hbm] * 8,
            out_specs=(in_hbm, in_hbm),
            scratch_shapes=[
                pltpu.VMEM((tokens, width), BF16),
                pltpu.VMEM((1, half), F32),
                pltpu.VMEM((slots, depth), BF16),
                pltpu.VMEM((depth, width), BF16),
                pltpu.VMEM((1, width), BF16),
                pltpu.VMEM((2,) + ids_fwd.shape[3:1:-1], jnp.int32),
                pltpu.VMEM((2,) + ids_fwd.shape[3:1:-1], F32),
                pltpu.VMEM((tokens, width), BF16),
                pltpu.VMEM((tokens, width), BF16),
                pltpu.VMEM((replicas, tokens, wide), BF16),
                pltpu.VMEM((replicas, tokens, wide), BF16),
                pltpu.VMEM(ids_fwd.shape[3:1:-1], jnp.int32),
                pltpu.VMEM(ids_fwd.shape[3:1:-1], F32),
                pltpu.VMEM((SIDE, 2 * SIDE, wide // 2), BF16),
                pltpu.VMEM((SIDE, 2 * SIDE, wide // 2), BF16),
                pltpu.VMEM((SIDE, ROWS, LANES), F32),
                pltpu.VMEM((SIDE, ROWS, LANES), F32),
                *(blocks * 4),
                pltpu.SemaphoreType.DMA((len(CHUNKS) + 7,)),
                pltpu.SemaphoreType.DMA((len(CHUNKS) + 1,)),
                pltpu.SemaphoreType.DMA((messages,)),
                pltpu.SemaphoreType.DMA((messages,)),
            ],
            compiler_params=pltpu.CompilerParams(
                collective_id=0, has_side_effects=True, vmem_limit_bytes=64 * 2**20
            ),
            cost_estimate=pl.CostEstimate(
                flops=2 * slots * depth * width,
                bytes_accessed=2 * (depth * width + slots * depth + 4 * tokens * width),
                transcendentals=0,
            ),
        )(
            carry,
            hidden,
            weight,
            bias,
            *(jnp.swapaxes(a, 2, 3) for a in (ids_fwd, gates_fwd, ids_bwd, gates_bwd)),
        )
        anywhere = pl.BlockSpec(memory_space=pl.ANY)
        return pl.pallas_call(
            hand_over,
            out_shape=shapes,
            in_specs=[anywhere] * 2,
            out_specs=(anywhere, anywhere),
            scratch_shapes=[
                *(pltpu.VMEM(shape.shape, shape.dtype) for shape in shapes),
                pltpu.SemaphoreType.DMA((4,)),
            ],
            compiler_params=pltpu.CompilerParams(vmem_limit_bytes=64 * 2**20),
        )(*results)

    placed = (
        P("section", "dp", "expert", None),
        P("section", "dp", "expert", None, None),
        P("section", "expert", None, None),
        P("section", "expert", None),
        P("section", "dp", "expert", None),
        P("section", "dp", "expert", None),
        P("section", "dp", "expert", None),
        P("section", "dp", "expert", None),
    )
    return jax.shard_map(
        step,
        mesh=mesh,
        in_specs=placed,
        out_specs=(P("section", "dp", "expert", None), P("section", "expert", "dp")),
        check_vma=False,
    )
```

time: 61.8 us -> 51.5 us (0.83)
  the two profiles are of different devices: /device:TPU:16 before, /device:TPU:1 now
where the time goes in v2:
time: 51.5 us; the launch traced here: 51.3 us
  Pallas kernels  50.7 us (98%)
  between operations  0.64 us (1%)
    pallas_call x1, Pallas kernels, step(): pl.pallas_call(functools.partial(kernel, cap, replicas, sections), out_sh...  49 us
    pallas_call x1, Pallas kernels, step(): pl.pallas_call(hand_over, out_shape=shapes, in_specs=[anywhere] * 2, out_...  1.64 us

profile of v2, /device:TPU:1, one launch (start us, length us, event | category | flops | bytes accessed | tf_op | source)
XLA Modules:
  0.0 51.3 jit_solution(3865442021390673628)
XLA Ops:
  0.6 49.0 %shard_map.95 = (bf16[1,1,64,1440]{3,2,1,0:T(8,128)(2,1)}, f32[1,1,720]{2,1,0:T(1,128)}) custom-call(bf16[2,1,64,1440]{3,2,1,0:T(8,128)(2,1)} %carry.1, bf16[1,1,1,320,1440]{4,3,2,1,0:T(8,128)(2,1)} %hidden.1, bf16[1,1,1440,1440]{3,2,1,0:T(8,128)(2,1)} %weight.1, bf16[1,1,1440]{2,1,0:T(2,128)(2,1)} %bias.1, s32[1,1,4,64]{3,2,1,0:T(4,128)} %bitcast.4, ...), custom_call_target="tpu_custom_call" | custom-call | flops 1327104000 | bytes 5806080 | tf_op jit(solution)/shard_map/pallas_call | solution.py:350
  49.7 1.6 %shard_map.96 = (bf16[1,1,64,1440]{3,2,1,0:T(8,128)(2,1)}, f32[1,1,720]{2,1,0:T(1,128)}) custom-call(bf16[1,1,64,1440]{3,2,1,0:T(8,128)(2,1)} %get-tuple-element.4.out, f32[1,1,720]{2,1,0:T(1,128)} %get-tuple-element.5.bias_grad), custom_call_target="tpu_custom_call" | custom-call | tf_op jit(solution)/shard_map/pallas_call | solution.py:395

commit v3 on v2

--- a/solution.py
+++ b/solution.py
@@ -14,13 +14,25 @@
 LANES = 128
 
 CHUNKS = (
-    (0, 256, "z"),
-    (768, 256, "x"),
-    (256, 256, "z"),
-    (1024, 256, "x"),
-    (512, 256, "z"),
+    (768, 512, "x"),
+    (0, 384, "z"),
     (1280, 160, "x"),
+    (384, 384, "z"),
 )
+
+TAIL = 32
+PARTS = LANES // TAIL
+
+
+def packed_rows(group):
+    return pl.cdiv(group // PARTS, 16) * 16
+
+
+def block_shape(group, size):
+    if size % LANES == 0:
+        return (group, size)
+    assert size == LANES + TAIL
+    return (packed_rows(group) + group, LANES)
 
 
 def iota(shape, dim):
@@ -200,17 +212,44 @@
         block = dot(hid_v[...], wgt_v[:, columns]) + bias_v[:, columns].astype(F32)
         if axis == "x":
             block = dot(swap, block.astype(BF16))
+        put(first_out[i], block)
+
+    tall, short = packed_rows(group), group // PARTS
+
+    def picks():
+        row, column = iota((SIDE * tall, slots), 0), iota((SIDE * tall, slots), 1)
+        inside = row & (tall - 1)
+        at = (row >> (tall.bit_length() - 1)) * group + inside
+        inside = inside < short
+        return [jnp.where(inside & (column == at + q * short), 1.0, 0.0).astype(BF16) for q in range(PARTS)]
+
+    pick = picks()
+
+    def put(ref, block):
+        whole = ref.shape[2]
+        above = ref.shape[1] - group
+        block = block.astype(BF16)
+        if above:
+            packed = jnp.concatenate([dot(p, block[:, whole:]) for p in pick], axis=1).astype(BF16)
         for other in range(SIDE):
-            first_out[i][other] = block[other * group : (other + 1) * group].astype(BF16)
+            ref[other, above:, :] = block[other * group : (other + 1) * group, :whole]
+            if above:
+                ref[other, :above, :] = packed[other * above : (other + 1) * above]
 
     def gathered(ref):
-        return ref[...].reshape(slots, ref.shape[2])
+        above = ref.shape[1] - group
+        rows = ref[:, above:, :].reshape(slots, ref.shape[2])
+        if not above:
+            return rows
+        packed = ref[:, :above, :].reshape(SIDE * above, ref.shape[2])
+        tail = jnp.zeros((slots, TAIL), F32)
+        for q, p in enumerate(pick):
+            tail = tail + dot(p, packed[:, q * TAIL : (q + 1) * TAIL], ((0,), (0,)))
+        return jnp.concatenate([rows, tail.astype(BF16)], axis=1)
 
     @jax.named_scope("turn")
     def turn(i):
-        block = dot(swap, gathered(first_in[i]))
-        for other in range(SIDE):
-            second_out[i][other] = block[other * group : (other + 1) * group].astype(BF16)
+        put(second_out[i], dot(swap, gathered(first_in[i])))
 
     per = SIDE - 1
     first_sem = [i * per for i in range(n)]
@@ -271,7 +310,7 @@
         axis = other_axis[CHUNKS[i][2]]
         second[i] = exchange(axis, second_out[i], second_in[i], second_sem[i])
 
-    for i in range(n):
+    for i in range(n - 2):
         second_phase(i)
 
     arrived(col_copies)
@@ -284,6 +323,9 @@
                     h * SIDE + other : h * SIDE + other + 1, tile * LANES : (tile + 1) * LANES
                 ]
     row_copies = exchange("z", row_out, row_in, row_sem)
+
+    for i in range(n - 2, n):
+        second_phase(i)
 
     @jax.named_scope("finish")
     def finish(i):
@@ -340,7 +382,9 @@
         cap = slots // experts
         half = width // replicas
         wide = pl.cdiv(half, 2 * LANES) * 2 * LANES
-        blocks = [pltpu.VMEM((SIDE, SIDE * cap, size), BF16) for _, size, _ in CHUNKS]
+        blocks = [
+            pltpu.VMEM((SIDE,) + block_shape(SIDE * cap, size), BF16) for _, size, _ in CHUNKS
+        ]
         messages = (2 * len(CHUNKS) + 2) * (SIDE - 1) + 5
         in_hbm = pl.BlockSpec(memory_space=pltpu.HBM)
         shapes = (

time: 51.5 us -> 50.4 us (0.979)
  Pallas kernels: 50.7 us -> 49.6 us
    pallas_call x1, Pallas kernels: 49 us -> 47.9 us  [step(): pl.pallas_call(functools.partial(kernel, cap, replicas, sections), out_sh...]
where the time goes in v3:
time: 50.4 us; the launch traced here: 50.2 us
  Pallas kernels  49.6 us (98%)
  between operations  0.64 us (1%)
    pallas_call x1, Pallas kernels, step(): pl.pallas_call(functools.partial(kernel, cap, replicas, sections), out_sh...  47.9 us
    pallas_call x1, Pallas kernels, step(): pl.pallas_call(hand_over, out_shape=shapes, in_specs=[anywhere] * 2, out_...  1.64 us

profile of v3, /device:TPU:1, one launch (start us, length us, event | category | flops | bytes accessed | tf_op | source)
XLA Modules:
  0.0 50.2 jit_solution(7941897525796621401)
XLA Ops:
  0.6 47.9 %shard_map.95 = (bf16[1,1,64,1440]{3,2,1,0:T(8,128)(2,1)}, f32[1,1,720]{2,1,0:T(1,128)}) custom-call(bf16[2,1,64,1440]{3,2,1,0:T(8,128)(2,1)} %carry.1, bf16[1,1,1,320,1440]{4,3,2,1,0:T(8,128)(2,1)} %hidden.1, bf16[1,1,1440,1440]{3,2,1,0:T(8,128)(2,1)} %weight.1, bf16[1,1,1440]{2,1,0:T(2,128)(2,1)} %bias.1, s32[1,1,4,64]{3,2,1,0:T(4,128)} %bitcast.4, ...), custom_call_target="tpu_custom_call" | custom-call | flops 1327104000 | bytes 5806080 | tf_op jit(solution)/shard_map/pallas_call | solution.py:394
  48.6 1.6 %shard_map.96 = (bf16[1,1,64,1440]{3,2,1,0:T(8,128)(2,1)}, f32[1,1,720]{2,1,0:T(1,128)}) custom-call(bf16[1,1,64,1440]{3,2,1,0:T(8,128)(2,1)} %get-tuple-element.4.out, f32[1,1,720]{2,1,0:T(1,128)} %get-tuple-element.5.bias_grad), custom_call_target="tpu_custom_call" | custom-call | tf_op jit(solution)/shard_map/pallas_call | solution.py:439
